TPU v7x, 256 devices: a whole 4x4x8 slice. The times are simulated.
256 devices in a mesh: row: 32 (over x, z), feat: 8 (over y, core).
Axes of the slice: x: 4, y: 4, z: 8, core: 2. Of those that a mesh axis runs over, the one named last changes fastest.
Arguments:
- candidates: bfloat16 [2048, 16384], P('row', 'feat'), may hold values from -48 to 48, as said below
- inv_factor: bfloat16 [16384, 16384], P('row', 'feat'), may hold values from -1.5 to 1.5, as said below
- weights: float32 [2048], P('row'), may hold values from 0.01 to 0.1
- strata: int32 [2048], P('row'), may hold values from 0 to 63, never falling along the last dimension, each value on 1 to 256 neighbouring positions
Outputs:
- new_weight: float32 [2048], P('row')
- leverage: float32 [2048], P('row')
- information: float32 [16384, 16384], P('row', 'feat')
Inputs may be any that keep to these rules, and one draw needn't show every extreme that they name: `candidates`: row scales and column scales differ. `inv_factor`: zero above the diagonal, positive on the diagonal.
All inputs are finite; a program needn't handle non-finite values.
Results may differ from a plain program's by a relative error of at most 0.0029.
Values may be sent and summed in bfloat16 or wider, within the bound.
A program may use at most 64 MiB of HBM per device.

v0:
```python
import jax
import jax.numpy as jnp
from jax import lax
from jax.sharding import PartitionSpec as P


def broadcast(shard, axis, root):
    mine = lax.axis_index(axis) == root
    return lax.psum(jnp.where(mine, shard, jnp.zeros_like(shard)), axis)


def per_device(candidates, inv_factor, weights, strata):
    rows_dev = candidates.shape[0]
    feat_block = candidates.shape[1]
    row_block = inv_factor.shape[0]
    row_count = lax.axis_size("row")
    feat_count = lax.axis_size("feat")
    features = feat_block * feat_count
    gathered = lax.all_gather(candidates, "row", axis=0, tiled=True)
    partial_value = lax.dot_general(
        gathered, inv_factor, (((1,), (1,)), ((), ())), preferred_element_type=jnp.float32
    )
    shaped = partial_value.reshape(row_count, rows_dev, row_block)
    summed = lax.psum_scatter(shaped, "feat", scatter_dimension=1, tiled=True)
    squares = jnp.sum(summed * summed, axis=2)
    reduced = lax.psum_scatter(squares, "row", scatter_dimension=0, tiled=True)
    raw_leverage = lax.all_gather(reduced, "feat", axis=1, tiled=True).reshape(rows_dev)
    leverage = raw_leverage / features
    strata_count = 2 * row_count
    membership = (strata[:, None] == jnp.arange(strata_count, dtype=jnp.int32)[None, :]).astype(
        jnp.float32
    )
    products = weights * raw_leverage
    local_product = lax.dot_general(
        membership, products, (((0,), (0,)), ((), ())), precision=lax.Precision.HIGHEST
    )
    local_mass = lax.dot_general(
        membership, weights, (((0,), (0,)), ((), ())), precision=lax.Precision.HIGHEST
    )
    stratum_product, stratum_mass = lax.psum((local_product, local_mass), "row")
    stratum_ratio = stratum_mass / stratum_product
    row_ratio = jnp.dot(membership, stratum_ratio, precision=lax.Precision.HIGHEST)
    new_weight = products * row_ratio
    weight_step = new_weight - weights
    step_all = lax.all_gather(weight_step, "row", axis=0, tiled=True)
    scaled_all = (step_all[:, None] * gathered.astype(jnp.float32)).astype(jnp.bfloat16)
    blocks_per_feat = row_count // feat_count
    row_index = lax.axis_index("row")
    offset = row_index % blocks_per_feat * row_block
    mine = lax.dynamic_slice_in_dim(gathered, offset, row_block, 1)
    root_index = row_index // blocks_per_feat
    column_block = broadcast(mine, "feat", root_index)
    information = lax.dot_general(
        column_block, scaled_all, (((0,), (0,)), ((), ())), preferred_element_type=jnp.float32
    )
    return (new_weight, leverage, information)


def solution(mesh):
    in_specs = (P("row", "feat"), P("row", "feat"), P("row"), P("row"))
    out_specs = (P("row"), P("row"), P("row", "feat"))
    return jax.shard_map(
        per_device, mesh=mesh, in_specs=in_specs, out_specs=out_specs, check_vma=False
    )
```

profile of v0, /device:TPU:0, one launch (start us, length us, event | category | flops | bytes accessed | tf_op | source)
XLA Modules:
  0.0 475.3 jit_solution(4714383224408392123)
XLA Ops:
  7.2 0.0 all-gather.2.cloned.1.call-start
  7.2 0.7 all-gather.2.cloned.1.call-update
  7.9 0.0 reduce-scatter.2.cloned.1.call-start
  8.0 102.2 %all-gather.2.cloned.1.call-done = bf16[2048,2048]{1,0:T(8,128)(2,1)} async-done(((bf16[64,2048]{1,0:T(8,128)(2,1)}), bf16[2048,2048]{1,0:T(8,128)(2,1)}) %all-gather.2.cloned.1.call-update) | async-done | bytes 8388624 | tf_op jit(solution)/shard_map/all_gather | solution.py:19
  110.2 9.5 %fusion.12 = f32[2048,512]{1,0:T(8,128)} fusion(bf16[2048,2048]{1,0:T(8,128)(2,1)} %all-gather.2.cloned.1.call-done, bf16[512,2048]{1,0:T(8,128)(2,1)S(1)} %copy-done), kind=kOutput, calls=%fused_computation.22 | convolution fusion | flops 4294967296 | bytes 14680064 | tf_op jit(solution)/shard_map/dot_general | solution.py:20
  119.7 0.0 reduce-scatter.2.cloned.1.call-update
  119.7 0.0 all-reduce.6.cloned.1.call-start
  119.8 3.3 dynamic-slice_select_fusion
  123.1 0.2 convolution_bitcast_fusion.2
  123.3 0.6 dynamic-slice
  124.6 0.6 fusion.11
  125.9 31.5 %reduce-scatter.2.cloned.1.call-done = f32[32,8,512]{2,1,0:T(8,128)} async-done(((f32[32,64,512]{2,1,0:T(8,128)}), f32[32,8,512]{2,1,0:T(8,128)}) %reduce-scatter.2.cloned.1.call-update) | async-done | bytes 524304 | tf_op jit(solution)/shard_map/reduce_scatter | solution.py:24
  157.4 1.2 multiply_reduce_fusion
  158.5 143.1 %all-reduce.2 = f32[32,8]{1,0:T(8,128)S(1)} all-reduce(f32[32,8]{1,0:T(8,128)S(1)} %multiply_reduce_fusion), channel_id=3, replica_groups=mesh['row'=32,'feat'=8] {'row'}, use_global_device_ids=true, to_apply=%region_2.0.clone | all-reduce | flops 256 | bytes 2048
  301.6 0.7 fusion.6
  302.3 12.4 %all-reduce = f32[64]{0:T(128)S(1)} all-reduce(f32[64]{0:T(128)S(1)} %fusion.6), channel_id=1, replica_groups=mesh['row'=32,'feat'=8] {'feat'}, use_global_device_ids=true, to_apply=%add | all-reduce | flops 64 | bytes 512 | tf_op jit(solution)/shard_map/reshape | solution.py:27
  314.7 0.5 broadcast_multiply_fusion
  315.2 0.2 convolution_bitcast_fusion.1
  315.4 69.6 %all-reduce.3 = (f32[64]{0:T(128)S(1)}, f32[64]{0:T(128)S(1)}) all-reduce(f32[64]{0:T(128)S(1)} %convolution_bitcast_fusion.2, f32[64]{0:T(128)S(1)} %convolution_bitcast_fusion.1), channel_id=1, replica_groups=mesh['row'=32,'feat'=8] {'row'}, use_global_device_ids=true, to_apply=%region_3.0 | all-reduce | flops 128 | bytes 1024 | tf_op jit(solution)/shard_map/psum | solution.py:40
  385.0 0.2 fusion.2
  385.2 0.1 subtract_dynamic-update-slice_fusion
  385.4 72.6 %all-reduce.1 = f32[2048]{0:T(1024)S(1)} all-reduce(f32[2048]{0:T(1024)S(1)} %subtract_dynamic-update-slice_fusion), channel_id=1, replica_groups=mesh['row'=32,'feat'=8] {'row'}, use_global_device_ids=true, to_apply=%add.1 | all-reduce | flops 2048 | bytes 16384
  458.0 0.0 all-reduce.6.cloned.1.call-done
  458.0 10.8 %fusion = f32[512,2048]{1,0:T(8,128)} fusion(bf16[2048,512]{1,0:T(8,128)(2,1)} %all-reduce.6.cloned.1.call-done, bf16[2048,2048]{1,0:T(8,128)(2,1)} %all-gather.2.cloned.1.call-done, f32[2048]{0:T(1024)S(1)} %all-reduce.1), kind=kOutput, calls=%fused_computation.1 | convolution fusion | flops 4307550208 | bytes 14688256 | tf_op jit(solution)/shard_map/dot_general | solution.py:53
  (15 shorter events, 0.1 us)
Async XLA Ops:
  7.2 103.0 %copy-start = (bf16[512,2048]{1,0:T(8,128)(2,1)S(1)}, bf16[512,2048]{1,0:T(8,128)(2,1)}, u32[]{:S(2)}) copy-start(bf16[512,2048]{1,0:T(8,128)(2,1)} %param.5) | copy-start | bytes 6291460
  7.2 103.0 %all-gather.2.cloned.1.call-start = ((), (), s32[]{:S(2)}) async-start(), calls=%async_computation.1 | async-start | bytes 8650752 | tf_op jit(solution)/shard_map/all_gather | solution.py:19
  7.9 149.5 %reduce-scatter.2.cloned.1.call-start = ((), (), s32[]{:S(2)}) async-start(), calls=%async_computation.2 | async-start | bytes 4718592 | tf_op jit(solution)/shard_map/reduce_scatter | solution.py:24
  119.7 3.4 copy-start.1
  119.7 3.4 copy-start.4
  119.7 3.6 copy-start.5
  119.7 4.8 %copy-start.2 = (u32[256]{0:T(256)S(1)}, u32[256]{0:T(256)}, u32[]{:S(2)}) copy-start(u32[256]{0:T(256)} %constant.54) | copy-start | bytes 3076
  119.7 338.3 %all-reduce.6.cloned.1.call-start = ((), (), s32[]{:S(2)}) async-start(), calls=%async_computation.3 | async-start | bytes 4194304 | tf_op jit(solution)/shard_map/psum | solution.py:9
  385.2 83.6 %copy-start.3 = (f32[64]{0:T(128)}, f32[64]{0:T(128)S(1)}, u32[]{:S(2)}) copy-start(f32[64]{0:T(128)S(1)} %fusion.2) | copy-start | bytes 772
Sparse Core Ops, SparseCore 0:
  10.6 99.5 all-gather.1
  119.8 37.5 reduce-scatter.1
  159.7 69.6 all-reduce.5
where the time goes:
time: 476 us; the launch traced here: 475 us
  blocking collectives  298 us (63%)
  waiting for transfers between devices  134 us (28%)
  matrix products  20.8 us (4%)
  between operations  15.2 us (3%)
  other arithmetic  5.06 us (1%)
    unnamed x2, blocking collectives  216 us
    all_gather x1, waiting for transfers between devices, per_device(): gathered = lax.all_gather(candidates, 'row', axis=0, tiled=True)  102 us
    psum x1, blocking collectives, per_device(): stratum_product, stratum_mass = lax.psum((local_product, local_mass), 'row')  69.6 us
    reduce_scatter x1, waiting for transfers between devices, per_device(): summed = lax.psum_scatter(shaped, 'feat', scatter_dimension=1, tiled=True)  31.5 us
    reshape x1, blocking collectives, per_device(): lax.all_gather(reduced, 'feat', axis=1, tiled=True).reshape(rows_dev)  12.4 us
    dot_general x1, matrix products, per_device(): lax.dot_general(column_block, scaled_all, (((0,), (0,)), ((), ())), prefe...  10.8 us
  transfers between devices with their start and end apart: 3, of which 2 were waited for; matrix products, arithmetic and copies ran while one was open for 2% of the time, Pallas kernels for 0%

commit v1 on v0

--- a/solution.py
+++ b/solution.py
@@ -2,6 +2,13 @@
 import jax.numpy as jnp
 from jax import lax
 from jax.sharding import PartitionSpec as P
+
+
+def all_by_exchange(array, mesh_axis, along):
+    peers = lax.axis_size(mesh_axis)
+    shards = jnp.stack([array for _ in range(peers)])
+    shards = lax.all_to_all(shards, mesh_axis, split_axis=0, concat_axis=0)
+    return jnp.concatenate(shards, axis=along)
 
 
 def broadcast(shard, axis, root):
@@ -16,7 +23,7 @@
     row_count = lax.axis_size("row")
     feat_count = lax.axis_size("feat")
     features = feat_block * feat_count
-    gathered = lax.all_gather(candidates, "row", axis=0, tiled=True)
+    gathered = all_by_exchange(candidates, "row", 0)
     partial_value = lax.dot_general(
         gathered, inv_factor, (((1,), (1,)), ((), ())), preferred_element_type=jnp.float32
     )

time: 476 us -> 570 us (1.20)
  blocking collectives: 298 us -> 493 us
  waiting for transfers between devices: 134 us -> 31.2 us
    all_to_all x0 -> x1, blocking collectives: none -> 195 us  [all_by_exchange(): shards = lax.all_to_all(shards, mesh_axis, split_axis=0, concat_axis=0)]
    all_gather x1 -> x0, waiting for transfers between devices: 102 us -> none  [per_device(): gathered = lax.all_gather(candidates, 'row', axis=0, tiled=True)]
  transfers between devices with their start and end apart: 3 -> 2, of which waited for: 2 -> 1; matrix products, arithmetic and copies ran while one was open for 2% -> 1% of each run, Pallas kernels for 0% -> 0%
where the time goes in v1:
time: 570 us
  blocking collectives  493 us (86%)
  waiting for transfers between devices  31.2 us (5%)
  matrix products  17.5 us (3%)
  between operations  15.5 us (3%)
  local copies, waits for them, and re-layouts  7.34 us (1%)
    unnamed x2, blocking collectives  216 us
    all_to_all x1, blocking collectives, all_by_exchange(): shards = lax.all_to_all(shards, mesh_axis, split_axis=0, concat_axis=0)  195 us
    psum x1, blocking collectives, per_device(): stratum_product, stratum_mass = lax.psum((local_product, local_mass), 'row')  69.6 us
    reduce_scatter x1, waiting for transfers between devices, per_device(): summed = lax.psum_scatter(shaped, 'feat', scatter_dimension=1, tiled=True)  31.2 us
    reshape x1, blocking collectives, per_device(): lax.all_gather(reduced, 'feat', axis=1, tiled=True).reshape(rows_dev)  12.4 us
  transfers between devices with their start and end apart: 2, of which 1 were waited for; matrix products, arithmetic and copies ran while one was open for 1% of the time, Pallas kernels for 0%

profile of v1, /device:TPU:0, one launch (start us, length us, event | category | flops | bytes accessed | tf_op | source)
XLA Modules:
  0.0 569.6 jit_solution(10725776341283185809)
XLA Ops:
  7.2 0.0 reduce-scatter.2.cloned.1.call-start
  7.2 2.1 stack.2
  9.4 195.3 %all_to_all.5 = bf16[32,64,2048]{2,1,0:T(8,128)(2,1)S(1)} all-to-all(bf16[32,64,2048]{2,1,0:T(8,128)(2,1)S(1)} %stack.2), channel_id=1, replica_groups=mesh['row'=32,'feat'=8] {'row'}, dimensions={0} | all-to-all | bytes 16777216 | tf_op jit(solution)/shard_map/all_to_all | solution.py:10
  204.7 3.2 copy-done.1
  207.9 6.1 %fusion.2 = f32[32,64,512]{2,1,0:T(8,128)} fusion(bf16[32,64,2048]{2,1,0:T(8,128)(2,1)S(1)} %all_to_all.5, bf16[512,2048]{1,0:T(8,128)(2,1)S(1)} %copy-done), kind=kOutput, calls=%fused_computation.3 | convolution fusion | flops 4294967296 | bytes 14680064 | tf_op jit(solution)/shard_map/dot_general | solution.py:27
  214.0 0.0 reduce-scatter.2.cloned.1.call-update
  214.1 0.0 all-reduce.6.cloned.1.call-start
  214.2 3.3 dynamic-slice_select_fusion
  217.5 0.2 convolution_bitcast_fusion.2
  217.7 0.6 dynamic-slice
  218.9 0.6 fusion.13
  220.2 31.2 %reduce-scatter.2.cloned.1.call-done = f32[32,8,512]{2,1,0:T(8,128)} async-done(((f32[32,64,512]{2,1,0:T(8,128)}), f32[32,8,512]{2,1,0:T(8,128)}) %reduce-scatter.2.cloned.1.call-update) | async-done | bytes 524304 | tf_op jit(solution)/shard_map/reduce_scatter | solution.py:31
  251.4 1.2 multiply_reduce_fusion
  252.5 143.0 %all-reduce.2 = f32[32,8]{1,0:T(8,128)S(1)} all-reduce(f32[32,8]{1,0:T(8,128)S(1)} %multiply_reduce_fusion), channel_id=3, replica_groups=mesh['row'=32,'feat'=8] {'row'}, use_global_device_ids=true, to_apply=%region_2.0.clone | all-reduce | flops 256 | bytes 2048
  395.6 0.7 fusion.8
  396.3 12.4 %all-reduce = f32[64]{0:T(128)S(1)} all-reduce(f32[64]{0:T(128)S(1)} %fusion.8), channel_id=1, replica_groups=mesh['row'=32,'feat'=8] {'feat'}, use_global_device_ids=true, to_apply=%add | all-reduce | flops 64 | bytes 512 | tf_op jit(solution)/shard_map/reshape | solution.py:34
  408.7 0.5 broadcast_multiply_fusion
  409.2 0.2 convolution_bitcast_fusion.1
  409.4 69.6 %all-reduce.3 = (f32[64]{0:T(128)S(1)}, f32[64]{0:T(128)S(1)}) all-reduce(f32[64]{0:T(128)S(1)} %convolution_bitcast_fusion.2, f32[64]{0:T(128)S(1)} %convolution_bitcast_fusion.1), channel_id=1, replica_groups=mesh['row'=32,'feat'=8] {'row'}, use_global_device_ids=true, to_apply=%region_3.0 | all-reduce | flops 128 | bytes 1024 | tf_op jit(solution)/shard_map/psum | solution.py:47
  479.0 0.2 fusion.4
  479.2 0.1 subtract_dynamic-update-slice_fusion
  479.3 72.6 %all-reduce.1 = f32[2048]{0:T(1024)S(1)} all-reduce(f32[2048]{0:T(1024)S(1)} %subtract_dynamic-update-slice_fusion), channel_id=1, replica_groups=mesh['row'=32,'feat'=8] {'row'}, use_global_device_ids=true, to_apply=%add.1 | all-reduce | flops 2048 | bytes 16384
  552.0 0.0 all-reduce.6.cloned.1.call-done
  552.0 10.8 %fusion = f32[512,2048]{1,0:T(8,128)} fusion(bf16[2048,512]{1,0:T(8,128)(2,1)} %all-reduce.6.cloned.1.call-done, bf16[2048,2048]{1,0:T(8,128)(2,1)} %bitcast.31, f32[2048]{0:T(1024)S(1)} %all-reduce.1), kind=kOutput, calls=%fused_computation.1 | convolution fusion | flops 4307550208 | bytes 14688256 | tf_op jit(solution)/shard_map/dot_general | solution.py:60
  (16 shorter events, 0.1 us)
Async XLA Ops:
  7.2 200.8 %copy-start = (bf16[512,2048]{1,0:T(8,128)(2,1)S(1)}, bf16[512,2048]{1,0:T(8,128)(2,1)}, u32[]{:S(2)}) copy-start(bf16[512,2048]{1,0:T(8,128)(2,1)} %param.5) | copy-start | bytes 6291460
  7.2 244.2 %reduce-scatter.2.cloned.1.call-start = ((), (), s32[]{:S(2)}) async-start(), calls=%async_computation.2 | async-start | bytes 4718592 | tf_op jit(solution)/shard_map/reduce_scatter | solution.py:31
  204.7 3.2 copy-start.1
  214.1 3.4 copy-start.2
  214.1 3.4 copy-start.5
  214.1 3.6 copy-start.6
  214.1 4.8 copy-start.3
  214.1 337.9 %all-reduce.6.cloned.1.call-start = ((), (), s32[]{:S(2)}) async-start(), calls=%async_computation.3 | async-start | bytes 4194304 | tf_op jit(solution)/shard_map/psum | solution.py:16
  479.2 83.6 %copy-start.4 = (f32[64]{0:T(128)}, f32[64]{0:T(128)S(1)}, u32[]{:S(2)}) copy-start(f32[64]{0:T(128)S(1)} %fusion.4) | copy-start | bytes 772
Sparse Core Ops, SparseCore 0:
  214.2 37.1 reduce-scatter.1
  253.7 69.9 all-reduce.5
